TPU v7x, 32 devices: a whole 2x2x4 slice. The times are simulated.
32 devices in a mesh: row: 8 (over y, x, core), col: 4 (over z).
Axes of the slice: x: 2, y: 2, z: 4, core: 2. Of those that a mesh axis runs over, the one named last changes fastest.
Arguments:
- features: bfloat16 [8192, 256], P(('row', 'col')), may hold values from -6 to 6
- out_degree: int32 [8192], P('row'), may hold values from 8 to 1024
- in_degree: int32 [8192], P('col'), may hold values from 8 to 1024
- tile_blocks: int32 [8, 4, 2, 128], P('row', 'col'), may hold values from 0 to 15, as said below
- tile_count: int32 [8, 4], P('row', 'col'), may hold values from 16 to 128, as said below
- tile_weights: bfloat16 [8, 4, 128, 128, 128], P('row', 'col'), may hold values from 0 to 4, as said below
- weight: bfloat16 [256, 256], replicated, may hold values from -0.375 to 0.375
- cotangent: bfloat16 [8192, 256], P(('col', 'row')), may hold values from -6 to 6
Outputs:
- hidden: bfloat16 [8192, 256], P(('col', 'row'))
- input_grad: bfloat16 [8192, 256], P(('row', 'col'))
- weight_grad: float32 [256, 256], replicated
Inputs may be any that keep to these rules, and one draw needn't show every extreme that they name: `tile_blocks`: entry [r, c, 0, s] is a target block below 16, entry [r, c, 1, s] a source block below 8; the pairs of one device position are distinct. `tile_count`: live tile slots of a device position are its first ones; some position has exactly 128. `tile_weights`: Non-negative edge weights.
All inputs are finite; a program needn't handle non-finite values.
Results may differ from a plain program's by a relative error of at most 0.0067.
Values may be sent and summed in bfloat16 or wider, within the bound.
A program may use at most 192 MiB of HBM per device.

v0:
```python
import functools

import jax
import jax.numpy as jnp
from jax import lax
from jax.experimental import pallas as pl
from jax.experimental.pallas import tpu as pltpu
from jax.sharding import PartitionSpec as P

TILE = 128
F32 = jnp.float32
BF16 = jnp.bfloat16
MESH = pl.DeviceIdType.MESH


def bit_orders(nr):
    bits = nr.bit_length() - 1
    return ([0] + list(range(1, bits)), [0] + list(range(bits - 1, 0, -1)))


class Group:
    def __init__(self, nr, me):
        self.nr, self.me = nr, me
        self.orders = bit_orders(nr)
        self.stages = len(self.orders[0])
        self.base = [nr - (nr >> s) for s in range(self.stages)]

    def bit(self, value, k):
        return (value // (1 << k)) % 2

    def partner(self, k):
        return self.me + (1 << k) * (1 - 2 * self.bit(self.me, k))

    def slot(self, half, stage, piece):
        rest = self.orders[half][stage + 1:]
        return self.base[stage] + sum(
            (self.bit(piece, b) * (1 << i) for i, b in enumerate(rest)), 0
        )

    def pieces(self, half, stage, mine):
        order = self.orders[half]
        own = sum((self.bit(self.me, b) * (1 << b) for b in order[:stage]), 0)
        k = order[stage]
        here = self.bit(self.me, k)
        here = here if mine else 1 - here
        rest = order[stage + 1:]
        return [
            own + here * (1 << k) + sum(((j >> i) & 1) << b for i, b in enumerate(rest))
            for j in range(1 << len(rest))
        ]


def kernel(
    nr, nc,
    feat_ref, odeg_ref, ideg_ref, blocks_ref, count_ref, tiles_hbm, w_ref, cot_ref,
    hid_ref, ig_ref, wg_ref,
    tiles, adj, adj_t, table_v, table_s, src, part, rs_out, rs_in, tg, zq_out, zq_in,
    wga_out, wga_in, wgb_in, wgc_in,
    loc_sem, tab_sem, zs_send, zs_recv, rs_send, rs_recv, ag_send, ag_recv,
    zq_send, zq_recv, wa_send, wa_recv, wb_send, wb_recv, wc_send, wc_recv,
):
    rows, hid = feat_ref.shape
    half_w = hid // 2
    sb, tb = nc * rows // TILE, nr * rows // TILE
    slots = tiles.shape[0]
    me_r, me_c = lax.axis_index("row"), lax.axis_index("col")
    group = Group(nr, me_r)
    row_id = lambda r: {"row": r, "col": me_c}
    col_id = lambda c: {"row": me_r, "col": c}

    def remote(src_ref, dst_ref, send, recv, where):
        return pltpu.make_async_remote_copy(
            src_ref=src_ref, dst_ref=dst_ref, send_sem=send, recv_sem=recv,
            device_id=where, device_id_type=MESH,
        )

    load_tiles = pltpu.make_async_copy(tiles_hbm, tiles, loc_sem)
    load_tiles.start()

    barrier = pltpu.get_barrier_semaphore()
    for d in range(1, nr):
        pl.semaphore_signal(
            barrier, inc=1, device_id=row_id(lax.rem(me_r + d, nr)), device_id_type=MESH
        )
    for d in range(1, nc):
        pl.semaphore_signal(
            barrier, inc=1, device_id=col_id(lax.rem(me_c + d, nc)), device_id_type=MESH
        )

    def scale_rows(deg_ref, first):
        cols = []
        for h in range(rows // TILE):
            deg = deg_ref[pl.ds(first + h, 1), :]
            line = lax.rsqrt(deg.astype(F32))
            cols.append(jnp.broadcast_to(line, (TILE, TILE)).T)
        return jnp.concatenate(cols, axis=0)

    out_scale = scale_rows(odeg_ref, me_c * (rows // TILE))
    for h in range(2):
        cut = slice(h * half_w, (h + 1) * half_w)
        src[h, me_c] = (feat_ref[:, cut].astype(F32) * out_scale).astype(BF16)

    pl.semaphore_wait(barrier, nr + nc - 2)

    def gather_copy(h, block, right):
        to = me_c + 1 if right else me_c - 1
        return remote(
            src.at[h, block], src.at[h, block],
            zs_send.at[0 if right else 1, h, block], zs_recv.at[h, block], col_id(to),
        )

    def gather_cases(k, right):
        block = me_c - k if right else me_c + k
        there = block >= 0 if right else block < nc
        on = me_c + 1 < nc if right else me_c >= 1
        return block, there, on

    def gather_step(k, h):
        for right in (True, False):
            block, there, on = gather_cases(k, right)
            if k > 0:
                @pl.when(there)
                def _():
                    gather_copy(h, block, right).wait_recv()
            if k < nc - 1:
                @pl.when(jnp.logical_and(there, on))
                def _():
                    gather_copy(h, block, right).start()

    def gather_drain(h):
        for k in range(nc - 1):
            for right in (True, False):
                block, there, on = gather_cases(k, right)

                @pl.when(jnp.logical_and(there, on))
                def _():
                    gather_copy(h, block, right).wait_send()

    for h in range(2):
        gather_step(0, h)

    flat = blocks_ref[0:1, :] * sb + blocks_ref[1:2, :]
    slot_line = lax.broadcasted_iota(jnp.int32, (1, slots), 1)
    flat = jnp.where(slot_line < count_ref[0, 0], flat, -1)
    down = jnp.broadcast_to(flat.astype(F32), (slots, slots)).T.astype(jnp.int32)
    slot_down = lax.broadcasted_iota(jnp.int32, (slots, slots), 0)
    lane = lax.broadcasted_iota(jnp.int32, (slots, slots), 1)
    for g in range(table_v.shape[0]):
        found = jnp.where(down == lane + g * slots, slot_down, -1)
        table_v[g:g + 1, :] = jnp.max(found, axis=0, keepdims=True)
    to_smem = pltpu.make_async_copy(table_v, table_s, tab_sem)
    to_smem.start()
    to_smem.wait()
    load_tiles.wait()

    def densify(t, carry):
        for s in range(sb):
            at = t * sb + s
            slot = table_s[at // slots, at % slots]
            tile = tiles[jnp.maximum(slot, 0)]
            tile = jnp.where(slot >= 0, tile, jnp.zeros_like(tile))
            adj[pl.ds(t * TILE, TILE), s * TILE:(s + 1) * TILE] = tile
            adj_t[t, s * TILE:(s + 1) * TILE, :] = tile.T
        return carry

    lax.fori_loop(0, tb, densify, 0)

    for k in range(1, nc):
        for h in range(2):
            gather_step(k, h)

    def rs_copy(h, stage, piece):
        slot = group.slot(h, stage, piece)
        return remote(
            rs_out.at[h, piece], rs_in.at[h, slot], rs_send.at[h, slot], rs_recv.at[h, slot],
            row_id(group.partner(group.orders[h][stage])),
        )

    def target_sums(piece):
        block = adj[pl.ds(pl.multiple_of(piece * rows, rows), rows), :]
        return [
            jnp.dot(block, src[h].reshape(nc * rows, half_w), preferred_element_type=F32)
            for h in range(2)
        ]

    for piece in group.pieces(0, 0, False):
        sums = target_sums(piece)
        for h in range(2):
            rs_out[h, piece] = sums[h].astype(BF16)
            rs_copy(h, 0, piece).start()
    for piece in group.pieces(0, 0, True):
        sums = target_sums(piece)
        for h in range(2):
            part[h, piece] = sums[h]

    for stage in range(1, group.stages):
        for h in range(2):
            for piece in group.pieces(h, stage, False):
                rs_copy(h, stage - 1, piece).wait_recv()
                got = rs_in[h, group.slot(h, stage - 1, piece)].astype(F32)
                rs_out[h, piece] = (part[h, piece] + got).astype(BF16)
                rs_copy(h, stage, piece).start()
        for h in range(2):
            for piece in group.pieces(h, stage, True):
                rs_copy(h, stage - 1, piece).wait_recv()
                got = rs_in[h, group.slot(h, stage - 1, piece)].astype(F32)
                part[h, piece] = part[h, piece] + got

    in_scale = scale_rows(ideg_ref, me_r * (rows // TILE))
    last = group.stages - 1
    totals = []
    for h in range(2):
        rs_copy(h, last, me_r).wait_recv()
        got = rs_in[h, group.slot(h, last, me_r)].astype(F32)
        totals.append(((part[h, me_r] + got) * in_scale).astype(BF16))
    agg = jnp.concatenate(totals, axis=1)
    pre_act = jnp.dot(agg, w_ref[...], preferred_element_type=F32)
    gate = jax.nn.sigmoid(pre_act)
    hid_ref[...] = (pre_act * gate).astype(BF16)
    slope = gate * (1.0 + pre_act * (1.0 - gate))
    pre_grad = (cot_ref[...].astype(F32) * slope).astype(BF16)
    back = lax.dot_general(
        pre_grad, w_ref[...], (((1,), (1,)), ((), ())), preferred_element_type=F32
    )

    def ag_copy(h, stage, piece):
        slot = group.slot(h, stage, piece)
        return remote(
            tg.at[h, piece], tg.at[h, piece], ag_send.at[h, slot], ag_recv.at[h, slot],
            row_id(group.partner(group.orders[h][stage])),
        )

    for h in range(2):
        tg[h, me_r] = (back[:, h * half_w:(h + 1) * half_w] * in_scale).astype(BF16)
        for stage in reversed(range(group.stages)):
            ag_copy(h, stage, me_r).start()

    wg_part = lax.dot_general(
        agg, pre_grad, (((0,), (0,)), ((), ())), preferred_element_type=F32
    )
    piece_rows = hid // nr
    wga_out[...] = wg_part.astype(BF16).reshape(nr, piece_rows, hid)

    def wa_copy(d):
        to = lax.rem(me_r + d, nr)
        return remote(
            wga_out.at[to], wga_in.at[d], wa_send.at[d], wa_recv.at[d], row_id(to)
        )

    def wb_copy(d):
        to = lax.rem(me_c + d, nc)
        return remote(
            wgb_in.at[me_c], wgb_in.at[me_c], wb_send.at[d], wb_recv.at[d], col_id(to)
        )

    def wb_arrival(d):
        frm = lax.rem(me_c + nc - d, nc)
        return remote(
            wgb_in.at[frm], wgb_in.at[frm], wb_send.at[d], wb_recv.at[d],
            col_id(lax.rem(me_c + d, nc)),
        )

    def wc_copy(d):
        to = lax.rem(me_r + d, nr)
        return remote(
            wgc_in.at[me_r], wgc_in.at[me_r], wc_send.at[d], wc_recv.at[d], row_id(to)
        )

    def wc_arrival(d):
        frm = lax.rem(me_r + nr - d, nr)
        return remote(
            wgc_in.at[frm], wgc_in.at[frm], wc_send.at[d], wc_recv.at[d],
            row_id(lax.rem(me_r + d, nr)),
        )

    def ag_receive(h, stage, piece):
        ag_copy(h, stage, piece).wait_recv()
        for onward in reversed(range(stage)):
            ag_copy(h, onward, piece).start()

    for stage in reversed(range(1, group.stages)):
        for h in range(2):
            for piece in group.pieces(h, stage, False):
                ag_receive(h, stage, piece)

    for d in range(1, nr):
        wa_copy(d).start()

    for h in range(2):
        for piece in group.pieces(h, 0, False):
            ag_receive(h, 0, piece)

    def zq_copy(h, dest, right):
        way = 0 if right else 1
        return remote(
            zq_out.at[h, dest], zq_in.at[way, h, dest], zq_send.at[h, dest],
            zq_recv.at[way, h, dest], col_id(me_c + 1 if right else me_c - 1),
        )

    def source_sums(dest):
        total = None
        at = pl.ds(pl.multiple_of(dest * rows, rows), rows)
        block = jnp.concatenate([adj_t[t, at, :] for t in range(tb)], axis=1)
        return [
            jnp.dot(block, tg[h].reshape(nr * rows, half_w), preferred_element_type=F32)
            for h in range(2)
        ]

    def stream(m, right):
        dest = me_c + m if right else me_c - m
        ok = dest < nc if right else dest >= 0
        upstream = me_c >= 1 if right else me_c + 1 < nc
        way = 0 if right else 1

        @pl.when(ok)
        def _():
            sums = source_sums(dest)
            for h in range(2):
                zq_out[h, dest] = sums[h].astype(BF16)

                @pl.when(upstream)
                def _():
                    zq_copy(h, dest, right).wait_recv()
                    got = zq_in[way, h, dest].astype(F32)
                    zq_out[h, dest] = (sums[h] + got).astype(BF16)

                zq_copy(h, dest, right).start()

    for m in range(nc - 1, 0, -1):
        for right in (True, False):
            stream(m, right)

    for d in range(1, nr):
        wa_copy(d).wait_recv()
    own = wga_out[me_r].astype(F32)
    for d in range(1, nr):
        own = own + wga_in[d].astype(F32)
    wgb_in[me_c] = own
    for d in range(1, nc):
        wb_copy(d).start()

    own_sums = source_sums(me_c)

    for d in range(1, nc):
        wb_arrival(d).wait_recv()
    total = wgb_in[0]
    for c in range(1, nc):
        total = total + wgb_in[c]
    wgc_in[me_r] = total
    for d in range(1, nr):
        wc_copy(d).start()

    for h in range(2):
        part[h, 0] = own_sums[h]
        for right in (True, False):
            there = me_c >= 1 if right else me_c + 1 < nc
            way = 0 if right else 1

            @pl.when(there)
            def _():
                zq_copy(h, me_c, right).wait_recv()
                part[h, 0] = part[h, 0] + zq_in[way, h, me_c].astype(F32)

        ig_ref[:, h * half_w:(h + 1) * half_w] = (part[h, 0] * out_scale).astype(BF16)

    for d in range(1, nr):
        wc_arrival(d).wait_recv()
    wg_ref[...] = wgc_in[...].reshape(hid, hid)

    for h in range(2):
        gather_drain(h)
        for stage in range(group.stages):
            for piece in group.pieces(h, stage, False):
                rs_copy(h, stage, piece).wait_send()
            for piece in group.pieces(h, stage, True):
                ag_copy(h, stage, piece).wait_send()
        for m in range(1, nc):
            @pl.when(me_c + m < nc)
            def _():
                zq_copy(h, me_c + m, True).wait_send()

            @pl.when(me_c - m >= 0)
            def _():
                zq_copy(h, me_c - m, False).wait_send()
    for d in range(1, nr):
        wa_copy(d).wait_send()
        wc_copy(d).wait_send()
    for d in range(1, nc):
        wb_copy(d).wait_send()


def shards(
    nr, nc,
    features, out_degree, in_degree, tile_blocks, tile_count, tile_weights, weight, cotangent
):
    rows, hid = features.shape
    half_w = hid // 2
    slots = tile_weights.shape[2]
    src_rows, tgt_rows = out_degree.shape[0], in_degree.shape[0]
    sb, tb = src_rows // TILE, tgt_rows // TILE
    vmem = pl.BlockSpec(memory_space=pltpu.VMEM)
    smem = pl.BlockSpec(memory_space=pltpu.SMEM)
    dma = pltpu.SemaphoreType.DMA
    table_rows = -(-sb * tb // slots)
    return pl.pallas_call(
        functools.partial(kernel, nr, nc),
        out_shape=(
            jax.ShapeDtypeStruct((rows, hid), BF16),
            jax.ShapeDtypeStruct((rows, hid), BF16),
            jax.ShapeDtypeStruct((hid, hid), F32),
        ),
        in_specs=[
            vmem, vmem, vmem, vmem, smem, pl.BlockSpec(memory_space=pl.ANY), vmem, vmem
        ],
        out_specs=(vmem, vmem, vmem),
        scratch_shapes=[
            pltpu.VMEM((slots, TILE, TILE), BF16),
            pltpu.VMEM((tgt_rows, src_rows), BF16),
            pltpu.VMEM((tb, src_rows, TILE), BF16),
            pltpu.VMEM((table_rows, slots), jnp.int32),
            pltpu.SMEM((table_rows, slots), jnp.int32),
            pltpu.VMEM((2, nc, rows, half_w), BF16),
            pltpu.VMEM((2, nr, rows, half_w), F32),
            pltpu.VMEM((2, nr, rows, half_w), BF16),
            pltpu.VMEM((2, nr - 1, rows, half_w), BF16),
            pltpu.VMEM((2, nr, rows, half_w), BF16),
            pltpu.VMEM((2, nc, rows, half_w), BF16),
            pltpu.VMEM((2, 2, nc, rows, half_w), BF16),
            pltpu.VMEM((nr, hid // nr, hid), BF16),
            pltpu.VMEM((nr, hid // nr, hid), BF16),
            pltpu.VMEM((nc, hid // nr, hid), F32),
            pltpu.VMEM((nr, hid // nr, hid), F32),
            dma, dma,
            dma((2, 2, nc)), dma((2, nc)),
            dma((2, nr - 1)), dma((2, nr - 1)),
            dma((2, nr - 1)), dma((2, nr - 1)),
            dma((2, nc)), dma((2, 2, nc)),
            dma((nr,)), dma((nr,)),
            dma((nc,)), dma((nc,)),
            dma((nr,)), dma((nr,)),
        ],
        compiler_params=pltpu.CompilerParams(
            collective_id=0, has_side_effects=True, vmem_limit_bytes=60 * 1024 * 1024
        ),
    )(
        features,
        out_degree.reshape(sb, TILE),
        in_degree.reshape(tb, TILE),
        tile_blocks[0, 0],
        tile_count,
        tile_weights[0, 0],
        weight,
        cotangent,
    )


def solution(mesh):
    nr, nc = mesh.shape["row"], mesh.shape["col"]
    placed = (
        P(("row", "col"), None),
        P("row"),
        P("col"),
        P("row", "col", None, None),
        P("row", "col"),
        P("row", "col", None, None, None),
        P(),
        P(("col", "row"), None),
    )
    return jax.shard_map(
        functools.partial(shards, nr, nc),
        mesh=mesh,
        in_specs=placed,
        out_specs=(P(("col", "row"), None), P(("row", "col"), None), P()),
        check_vma=False,
    )
```

profile of v0, /device:TPU:0, one launch (start us, length us, event | category | flops | bytes accessed | tf_op | source)
XLA Modules:
  0.0 67.2 jit_solution(8707843833696116833)
XLA Ops:
  1.3 61.1 %shard_map.103 = (bf16[256,256]{1,0:T(8,128)(2,1)}, bf16[256,256]{1,0:T(8,128)(2,1)}, f32[256,256]{1,0:T(8,128)}) custom-call(bf16[256,256]{1,0:T(8,128)(2,1)} %feat_ref.1, s32[8,128]{1,0:T(8,128)} %bitcast.6, s32[16,128]{1,0:T(8,128)} %bitcast.5, s32[2,128]{1,0:T(2,128)} %bitcast.7, s32[1,1]{1,0:T(1,128)S(6)} %copy.14.count_ref, ...), custom_call_target="tpu_custom_call" | custom-call | tf_op jit(solution)/shard_map/pallas_call | solution.py:405
  62.4 1.6 %copy.15 = bf16[256,256]{1,0:T(8,128)(2,1)} copy(bf16[256,256]{1,0:T(8,128)(2,1)} %get-tuple-element.6) | data formatting | bytes 262144
  63.9 1.6 %copy.16 = bf16[256,256]{1,0:T(8,128)(2,1)} copy(bf16[256,256]{1,0:T(8,128)(2,1)} %get-tuple-element.7) | data formatting | bytes 262144
  65.5 1.7 %copy.17 = f32[256,256]{1,0:T(8,128)} copy(f32[256,256]{1,0:T(8,128)} %get-tuple-element.8) | data formatting | bytes 524288
where the time goes:
time: 67.4 us; the launch traced here: 67.2 us
  Pallas kernels  61.1 us (91%)
  local copies, waits for them, and re-layouts  4.8 us (7%)
  between operations  1.29 us (2%)
    pallas_call x1, Pallas kernels, shards(): pl.pallas_call(functools.partial(kernel, nr, nc), out_shape=(jax.ShapeDty...  61.1 us
    unnamed x3, local copies, waits for them, and re-layouts  4.8 us

commit v1 on v0

--- a/solution.py
+++ b/solution.py
@@ -52,12 +52,14 @@
 
 def kernel(
     nr, nc,
-    feat_ref, odeg_ref, ideg_ref, blocks_ref, count_ref, tiles_hbm, w_ref, cot_ref,
-    hid_ref, ig_ref, wg_ref,
-    tiles, adj, adj_t, table_v, table_s, src, part, rs_out, rs_in, tg, zq_out, zq_in,
+    feat_hbm, odeg_hbm, ideg_hbm, blocks_hbm, count_hbm, tiles_hbm, w_hbm, cot_hbm,
+    hid_hbm, ig_hbm, wg_hbm,
+    feat_ref, odeg_ref, ideg_ref, blocks_ref, count_ref, w_ref, cot_ref, hid_ref, ig_ref,
+    in_sem, out_sem,
+    tiles, adj, adj_t, table_v, table_s, src, part, rs_out, rs_in, tg, zq_out, zq_in, zq_fin,
     wga_out, wga_in, wgb_in, wgc_in,
     loc_sem, tab_sem, zs_send, zs_recv, rs_send, rs_recv, ag_send, ag_recv,
-    zq_send, zq_recv, wa_send, wa_recv, wb_send, wb_recv, wc_send, wc_recv,
+    zq_send, zq_recv, zf_recv, wa_send, wa_recv, wb_send, wb_recv, wc_send, wc_recv,
 ):
     rows, hid = feat_ref.shape
     half_w = hid // 2
@@ -74,9 +76,6 @@
             device_id=where, device_id_type=MESH,
         )
 
-    load_tiles = pltpu.make_async_copy(tiles_hbm, tiles, loc_sem)
-    load_tiles.start()
-
     barrier = pltpu.get_barrier_semaphore()
     for d in range(1, nr):
         pl.semaphore_signal(
@@ -86,6 +85,20 @@
         pl.semaphore_signal(
             barrier, inc=1, device_id=col_id(lax.rem(me_c + d, nc)), device_id_type=MESH
         )
+
+    loads = [
+        pltpu.make_async_copy(a, b, in_sem.at[i])
+        for i, (a, b) in enumerate([
+            (feat_hbm, feat_ref), (odeg_hbm, odeg_ref), (blocks_hbm, blocks_ref),
+            (count_hbm, count_ref), (ideg_hbm, ideg_ref), (w_hbm, w_ref), (cot_hbm, cot_ref),
+        ])
+    ]
+    load_tiles = pltpu.make_async_copy(tiles_hbm, tiles, loc_sem)
+    for load in loads:
+        load.start()
+    load_tiles.start()
+    loads[0].wait()
+    loads[1].wait()
 
     def scale_rows(deg_ref, first):
         cols = []
@@ -102,46 +115,43 @@
 
     pl.semaphore_wait(barrier, nr + nc - 2)
 
-    def gather_copy(h, block, right):
-        to = me_c + 1 if right else me_c - 1
+    def gather_copy(h, block, hops, right, at):
+        to = me_c + hops if right else me_c - hops
         return remote(
             src.at[h, block], src.at[h, block],
-            zs_send.at[0 if right else 1, h, block], zs_recv.at[h, block], col_id(to),
-        )
-
-    def gather_cases(k, right):
-        block = me_c - k if right else me_c + k
-        there = block >= 0 if right else block < nc
-        on = me_c + 1 < nc if right else me_c >= 1
-        return block, there, on
-
-    def gather_step(k, h):
+            zs_send.at[0 if right else 1, h, at], zs_recv.at[h, block], col_id(to),
+        )
+
+    def inside(step, right):
+        return me_c + step < nc if right else me_c >= step
+
+    def gather_own(h, act):
+        for hops in (2, 1):
+            for right in (True, False):
+                @pl.when(inside(hops, right))
+                def _():
+                    act(gather_copy(h, me_c, hops, right, hops - 1))
+
+    def gather_onward(h, k, act):
         for right in (True, False):
-            block, there, on = gather_cases(k, right)
-            if k > 0:
-                @pl.when(there)
-                def _():
-                    gather_copy(h, block, right).wait_recv()
-            if k < nc - 1:
-                @pl.when(jnp.logical_and(there, on))
-                def _():
-                    gather_copy(h, block, right).start()
-
-    def gather_drain(h):
-        for k in range(nc - 1):
-            for right in (True, False):
-                block, there, on = gather_cases(k, right)
-
-                @pl.when(jnp.logical_and(there, on))
-                def _():
-                    gather_copy(h, block, right).wait_send()
-
-    for h in range(2):
-        gather_step(0, h)
-
+            @pl.when(jnp.logical_and(inside(k, not right), inside(1, right)))
+            def _():
+                act(gather_copy(h, me_c - k if right else me_c + k, 1, right, k))
+
+    def gather_arrived(h, k):
+        for right in (True, False):
+            @pl.when(inside(k, not right))
+            def _():
+                gather_copy(h, me_c - k if right else me_c + k, 1, right, k).wait_recv()
+
+    for h in range(2):
+        gather_own(h, lambda c: c.start())
+
+    loads[2].wait()
+    loads[3].wait()
     flat = blocks_ref[0:1, :] * sb + blocks_ref[1:2, :]
     slot_line = lax.broadcasted_iota(jnp.int32, (1, slots), 1)
-    flat = jnp.where(slot_line < count_ref[0, 0], flat, -1)
+    flat = jnp.where(slot_line < count_ref[...], flat, -1)
     down = jnp.broadcast_to(flat.astype(F32), (slots, slots)).T.astype(jnp.int32)
     slot_down = lax.broadcasted_iota(jnp.int32, (slots, slots), 0)
     lane = lax.broadcasted_iota(jnp.int32, (slots, slots), 1)
@@ -165,9 +175,12 @@
 
     lax.fori_loop(0, tb, densify, 0)
 
-    for k in range(1, nc):
-        for h in range(2):
-            gather_step(k, h)
+    for k in range(2, nc):
+        for h in range(2):
+            gather_arrived(h, k)
+            gather_onward(h, k, lambda c: c.start())
+    for h in range(2):
+        gather_arrived(h, 1)
 
     def rs_copy(h, stage, piece):
         slot = group.slot(h, stage, piece)
@@ -206,6 +219,8 @@
                 got = rs_in[h, group.slot(h, stage - 1, piece)].astype(F32)
                 part[h, piece] = part[h, piece] + got
 
+    for load in loads[4:]:
+        load.wait()
     in_scale = scale_rows(ideg_ref, me_r * (rows // TILE))
     last = group.stages - 1
     totals = []
@@ -217,6 +232,8 @@
     pre_act = jnp.dot(agg, w_ref[...], preferred_element_type=F32)
     gate = jax.nn.sigmoid(pre_act)
     hid_ref[...] = (pre_act * gate).astype(BF16)
+    store_hid = pltpu.make_async_copy(hid_ref, hid_hbm, out_sem.at[0])
+    store_hid.start()
     slope = gate * (1.0 + pre_act * (1.0 - gate))
     pre_grad = (cot_ref[...].astype(F32) * slope).astype(BF16)
     back = lax.dot_general(
@@ -290,15 +307,30 @@
         for piece in group.pieces(h, 0, False):
             ag_receive(h, 0, piece)
 
-    def zq_copy(h, dest, right):
+    def zq_copy(h, hops, right):
+        way, step = (0, 1) if right else (1, -1)
+        dest = me_c + step * hops
+        if hops <= 2:
+            into, sem, to = zq_fin.at[way, hops - 1, h], zf_recv.at[way, hops - 1, h], dest
+        else:
+            into, sem, to = zq_in.at[way, h, dest], zq_recv.at[way, h, dest], me_c + step
+        return remote(zq_out.at[h, dest], into, zq_send.at[h, dest], sem, col_id(to))
+
+    def zq_relayed(h, dest, right):
         way = 0 if right else 1
         return remote(
             zq_out.at[h, dest], zq_in.at[way, h, dest], zq_send.at[h, dest],
-            zq_recv.at[way, h, dest], col_id(me_c + 1 if right else me_c - 1),
+            zq_recv.at[way, h, dest], col_id(dest),
+        )
+
+    def zq_final(h, hops, right):
+        way = 0 if right else 1
+        return remote(
+            zq_out.at[h, me_c], zq_fin.at[way, hops - 1, h], zq_send.at[h, me_c],
+            zf_recv.at[way, hops - 1, h], col_id(me_c + 1 if right else me_c - 1),
         )
 
     def source_sums(dest):
-        total = None
         at = pl.ds(pl.multiple_of(dest * rows, rows), rows)
         block = jnp.concatenate([adj_t[t, at, :] for t in range(tb)], axis=1)
         return [
@@ -308,27 +340,27 @@
 
     def stream(m, right):
         dest = me_c + m if right else me_c - m
-        ok = dest < nc if right else dest >= 0
-        upstream = me_c >= 1 if right else me_c + 1 < nc
         way = 0 if right else 1
 
-        @pl.when(ok)
+        @pl.when(inside(m, right))
         def _():
             sums = source_sums(dest)
             for h in range(2):
                 zq_out[h, dest] = sums[h].astype(BF16)
-
-                @pl.when(upstream)
-                def _():
-                    zq_copy(h, dest, right).wait_recv()
-                    got = zq_in[way, h, dest].astype(F32)
-                    zq_out[h, dest] = (sums[h] + got).astype(BF16)
-
-                zq_copy(h, dest, right).start()
-
-    for m in range(nc - 1, 0, -1):
+                if m >= 2:
+                    @pl.when(inside(1, not right))
+                    def _():
+                        zq_relayed(h, dest, right).wait_recv()
+                        got = zq_in[way, h, dest].astype(F32)
+                        zq_out[h, dest] = (sums[h] + got).astype(BF16)
+
+                zq_copy(h, m, right).start()
+
+    for m in range(nc - 1, 2, -1):
         for right in (True, False):
             stream(m, right)
+    for right in (True, False):
+        stream(1, right)
 
     for d in range(1, nr):
         wa_copy(d).wait_recv()
@@ -339,7 +371,12 @@
     for d in range(1, nc):
         wb_copy(d).start()
 
+    for right in (True, False):
+        stream(2, right)
+
     own_sums = source_sums(me_c)
+    for h in range(2):
+        part[h, 0] = own_sums[h]
 
     for d in range(1, nc):
         wb_arrival(d).wait_recv()
@@ -350,43 +387,54 @@
     for d in range(1, nr):
         wc_copy(d).start()
 
-    for h in range(2):
-        part[h, 0] = own_sums[h]
-        for right in (True, False):
-            there = me_c >= 1 if right else me_c + 1 < nc
-            way = 0 if right else 1
-
-            @pl.when(there)
-            def _():
-                zq_copy(h, me_c, right).wait_recv()
-                part[h, 0] = part[h, 0] + zq_in[way, h, me_c].astype(F32)
-
+    for hops in (1, 2):
+        for h in range(2):
+            for right in (True, False):
+                way = 0 if right else 1
+
+                @pl.when(inside(hops, not right))
+                def _():
+                    zq_final(h, hops, right).wait_recv()
+                    part[h, 0] = part[h, 0] + zq_fin[way, hops - 1, h].astype(F32)
+
+    for h in range(2):
         ig_ref[:, h * half_w:(h + 1) * half_w] = (part[h, 0] * out_scale).astype(BF16)
+    store_ig = pltpu.make_async_copy(ig_ref, ig_hbm, out_sem.at[1])
+    store_ig.start()
 
     for d in range(1, nr):
         wc_arrival(d).wait_recv()
-    wg_ref[...] = wgc_in[...].reshape(hid, hid)
-
-    for h in range(2):
-        gather_drain(h)
+    store_wg = pltpu.make_async_copy(wgc_in, wg_hbm, out_sem.at[2])
+    store_wg.start()
+
+    for h in range(2):
+        gather_own(h, lambda c: c.wait_send())
+        for k in range(2, nc):
+            gather_onward(h, k, lambda c: c.wait_send())
         for stage in range(group.stages):
             for piece in group.pieces(h, stage, False):
                 rs_copy(h, stage, piece).wait_send()
             for piece in group.pieces(h, stage, True):
                 ag_copy(h, stage, piece).wait_send()
         for m in range(1, nc):
-            @pl.when(me_c + m < nc)
-            def _():
-                zq_copy(h, me_c + m, True).wait_send()
-
-            @pl.when(me_c - m >= 0)
-            def _():
-                zq_copy(h, me_c - m, False).wait_send()
+            for right in (True, False):
+                @pl.when(inside(m, right))
+                def _():
+                    zq_copy(h, m, right).wait_send()
     for d in range(1, nr):
         wa_copy(d).wait_send()
         wc_copy(d).wait_send()
     for d in range(1, nc):
         wb_copy(d).wait_send()
+    store_hid.wait()
+    store_ig.wait()
+    store_wg.wait()
+
+
+def place(hid_in, ig_in, wg_in, hid_out, ig_out, wg_out):
+    hid_out[...] = hid_in[...]
+    ig_out[...] = ig_in[...]
+    wg_out[...] = wg_in[...]
 
 
 def shards(
@@ -398,22 +446,30 @@
     slots = tile_weights.shape[2]
     src_rows, tgt_rows = out_degree.shape[0], in_degree.shape[0]
     sb, tb = src_rows // TILE, tgt_rows // TILE
-    vmem = pl.BlockSpec(memory_space=pltpu.VMEM)
-    smem = pl.BlockSpec(memory_space=pltpu.SMEM)
+    anywhere = pl.BlockSpec(memory_space=pl.ANY)
     dma = pltpu.SemaphoreType.DMA
     table_rows = -(-sb * tb // slots)
-    return pl.pallas_call(
+    out_shape = (
+        jax.ShapeDtypeStruct((rows, hid), BF16),
+        jax.ShapeDtypeStruct((rows, hid), BF16),
+        jax.ShapeDtypeStruct((nr, hid // nr, hid), F32),
+    )
+    results = pl.pallas_call(
         functools.partial(kernel, nr, nc),
-        out_shape=(
-            jax.ShapeDtypeStruct((rows, hid), BF16),
-            jax.ShapeDtypeStruct((rows, hid), BF16),
-            jax.ShapeDtypeStruct((hid, hid), F32),
-        ),
-        in_specs=[
-            vmem, vmem, vmem, vmem, smem, pl.BlockSpec(memory_space=pl.ANY), vmem, vmem
-        ],
-        out_specs=(vmem, vmem, vmem),
+        out_shape=out_shape,
+        in_specs=[anywhere] * 8,
+        out_specs=(anywhere,) * 3,
         scratch_shapes=[
+            pltpu.VMEM((rows, hid), BF16),
+            pltpu.VMEM((sb, TILE), jnp.int32),
+            pltpu.VMEM((tb, TILE), jnp.int32),
+            pltpu.VMEM((2, slots), jnp.int32),
+            pltpu.VMEM((1, 1), jnp.int32),
+            pltpu.VMEM((hid, hid), BF16),
+            pltpu.VMEM((rows, hid), BF16),
+            pltpu.VMEM((rows, hid), BF16),
+            pltpu.VMEM((rows, hid), BF16),
+            dma((7,)), dma((3,)),
             pltpu.VMEM((slots, TILE, TILE), BF16),
             pltpu.VMEM((tgt_rows, src_rows), BF16),
             pltpu.VMEM((tb, src_rows, TILE), BF16),
@@ -426,6 +482,7 @@
             pltpu.VMEM((2, nr, rows, half_w), BF16),
             pltpu.VMEM((2, nc, rows, half_w), BF16),
             pltpu.VMEM((2, 2, nc, rows, half_w), BF16),
+            pltpu.VMEM((2, 2, 2, rows, half_w), BF16),
             pltpu.VMEM((nr, hid // nr, hid), BF16),
             pltpu.VMEM((nr, hid // nr, hid), BF16),
             pltpu.VMEM((nc, hid // nr, hid), F32),
@@ -434,7 +491,7 @@
             dma((2, 2, nc)), dma((2, nc)),
             dma((2, nr - 1)), dma((2, nr - 1)),
             dma((2, nr - 1)), dma((2, nr - 1)),
-            dma((2, nc)), dma((2, 2, nc)),
+            dma((2, nc)), dma((2, 2, nc)), dma((2, 2, 2)),
             dma((nr,)), dma((nr,)),
             dma((nc,)), dma((nc,)),
             dma((nr,)), dma((nr,)),
@@ -452,6 +509,13 @@
         weight,
         cotangent,
     )
+    hidden, input_grad, weight_grad = pl.pallas_call(
+        place,
+        out_shape=out_shape,
+        in_specs=[pl.BlockSpec(memory_space=pltpu.VMEM)] * 3,
+        out_specs=(pl.BlockSpec(memory_space=pltpu.VMEM),) * 3,
+    )(*results)
+    return hidden, input_grad, weight_grad.reshape(hid, hid)
 
 
 def solution(mesh):

time: 67.4 us -> 55.7 us (0.83)
  Pallas kernels: 61.1 us -> 54.2 us
  local copies, waits for them, and re-layouts: 4.8 us -> 0 us
    pallas_call x1 -> x2, Pallas kernels: 61.1 us -> 54.2 us  [the longest x1 52.3 us: shards(): pl.pallas_call(functools.partial(kernel, nr, nc), out_shape=out_shape, in...]
    unnamed x3 -> x0, local copies, waits for them, and re-layouts: 4.8 us -> none
where the time goes in v1:
time: 55.7 us; the launch traced here: 55.5 us
  Pallas kernels  54.2 us (97%)
  between operations  1.29 us (2%)
    pallas_call x1, Pallas kernels, shards(): pl.pallas_call(functools.partial(kernel, nr, nc), out_shape=out_shape, in...  52.3 us
    pallas_call x1, Pallas kernels, shards(): pl.pallas_call(place, out_shape=out_shape, in_specs=[pl.BlockSpec(memory_...  1.88 us

profile of v1, /device:TPU:0, one launch (start us, length us, event | category | flops | bytes accessed | tf_op | source)
XLA Modules:
  0.0 55.5 jit_solution(18088625213836849926)
XLA Ops:
  1.3 52.3 %shard_map.103 = (bf16[256,256]{1,0:T(8,128)(2,1)}, bf16[256,256]{1,0:T(8,128)(2,1)}, f32[8,32,256]{2,1,0:T(8,128)}) custom-call(bf16[256,256]{1,0:T(8,128)(2,1)} %feat_hbm.1, s32[8,128]{1,0:T(8,128)} %bitcast.7, s32[16,128]{1,0:T(8,128)} %bitcast.6, s32[2,128]{1,0:T(2,128)} %bitcast.8, s32[1,1]{1,0:T(1,128)S(6)} %copy.11.count_hbm, ...), custom_call_target="tpu_custom_call" | custom-call | tf_op jit(solution)/shard_map/pallas_call | solution.py:457
  53.6 1.9 %shard_map.104 = (bf16[256,256]{1,0:T(8,128)(2,1)}, bf16[256,256]{1,0:T(8,128)(2,1)}, f32[8,32,256]{2,1,0:T(8,128)}) custom-call(bf16[256,256]{1,0:T(8,128)(2,1)} %get-tuple-element.9.hid_in, bf16[256,256]{1,0:T(8,128)(2,1)} %get-tuple-element.10.ig_in, f32[8,32,256]{2,1,0:T(8,128)} %get-tuple-element.11.wg_in), custom_call_target="tpu_custom_call" | custom-call | tf_op jit(solution)/shard_map/pallas_call | solution.py:512

commit v2 on v1

--- a/solution.py
+++ b/solution.py
@@ -37,7 +37,7 @@
             (self.bit(piece, b) * (1 << i) for i, b in enumerate(rest)), 0
         )
 
-    def pieces(self, half, stage, mine):
+    def pieces(self, half, stage, mine, near_first=False):
         order = self.orders[half]
         own = sum((self.bit(self.me, b) * (1 << b) for b in order[:stage]), 0)
         k = order[stage]
@@ -45,8 +45,11 @@
         here = here if mine else 1 - here
         rest = order[stage + 1:]
         return [
-            own + here * (1 << k) + sum(((j >> i) & 1) << b for i, b in enumerate(rest))
-            for j in range(1 << len(rest))
+            own + here * (1 << k) + sum(
+                ((self.bit(self.me, b) + (j >> i) % 2) % 2 * (1 << b) for i, b in enumerate(rest)),
+                0,
+            )
+            for j in (range(1 << len(rest)) if near_first else reversed(range(1 << len(rest))))
         ]
 
 
@@ -189,12 +192,14 @@
             row_id(group.partner(group.orders[h][stage])),
         )
 
+    def both_halves(block, held, depth):
+        full = jnp.concatenate([held[h].reshape(depth, half_w) for h in range(2)], axis=1)
+        sums = jnp.dot(block, full, preferred_element_type=F32)
+        return [sums[:, h * half_w:(h + 1) * half_w] for h in range(2)]
+
     def target_sums(piece):
         block = adj[pl.ds(pl.multiple_of(piece * rows, rows), rows), :]
-        return [
-            jnp.dot(block, src[h].reshape(nc * rows, half_w), preferred_element_type=F32)
-            for h in range(2)
-        ]
+        return both_halves(block, src, nc * rows)
 
     for piece in group.pieces(0, 0, False):
         sums = target_sums(piece)
@@ -297,14 +302,14 @@
 
     for stage in reversed(range(1, group.stages)):
         for h in range(2):
-            for piece in group.pieces(h, stage, False):
+            for piece in group.pieces(h, stage, False, near_first=True):
                 ag_receive(h, stage, piece)
 
     for d in range(1, nr):
         wa_copy(d).start()
 
     for h in range(2):
-        for piece in group.pieces(h, 0, False):
+        for piece in group.pieces(h, 0, False, near_first=True):
             ag_receive(h, 0, piece)
 
     def zq_copy(h, hops, right):
@@ -333,10 +338,7 @@
     def source_sums(dest):
         at = pl.ds(pl.multiple_of(dest * rows, rows), rows)
         block = jnp.concatenate([adj_t[t, at, :] for t in range(tb)], axis=1)
-        return [
-            jnp.dot(block, tg[h].reshape(nr * rows, half_w), preferred_element_type=F32)
-            for h in range(2)
-        ]
+        return both_halves(block, tg, nr * rows)
 
     def stream(m, right):
         dest = me_c + m if right else me_c - m

time: 55.7 us -> 53.8 us (0.966)
  Pallas kernels: 54.2 us -> 52.3 us
    pallas_call x1, Pallas kernels: 52.3 us -> 50.5 us  [shards(): pl.pallas_call(functools.partial(kernel, nr, nc), out_shape=out_shape, in...]
where the time goes in v2:
time: 53.8 us; the launch traced here: 53.6 us
  Pallas kernels  52.3 us (97%)
  between operations  1.29 us (2%)
    pallas_call x1, Pallas kernels, shards(): pl.pallas_call(functools.partial(kernel, nr, nc), out_shape=out_shape, in...  50.5 us
    pallas_call x1, Pallas kernels, shards(): pl.pallas_call(place, out_shape=out_shape, in_specs=[pl.BlockSpec(memory_...  1.88 us

profile of v2, /device:TPU:0, one launch (start us, length us, event | category | flops | bytes accessed | tf_op | source)
XLA Modules:
  0.0 53.6 jit_solution(127122275806813315)
XLA Ops:
  1.3 50.5 %shard_map.103 = (bf16[256,256]{1,0:T(8,128)(2,1)}, bf16[256,256]{1,0:T(8,128)(2,1)}, f32[8,32,256]{2,1,0:T(8,128)}) custom-call(bf16[256,256]{1,0:T(8,128)(2,1)} %feat_hbm.1, s32[8,128]{1,0:T(8,128)} %bitcast.7, s32[16,128]{1,0:T(8,128)} %bitcast.6, s32[2,128]{1,0:T(2,128)} %bitcast.8, s32[1,1]{1,0:T(1,128)S(6)} %copy.11.count_hbm, ...), custom_call_target="tpu_custom_call" | custom-call | tf_op jit(solution)/shard_map/pallas_call | solution.py:459
  51.7 1.9 %shard_map.104 = (bf16[256,256]{1,0:T(8,128)(2,1)}, bf16[256,256]{1,0:T(8,128)(2,1)}, f32[8,32,256]{2,1,0:T(8,128)}) custom-call(bf16[256,256]{1,0:T(8,128)(2,1)} %get-tuple-element.9.hid_in, bf16[256,256]{1,0:T(8,128)(2,1)} %get-tuple-element.10.ig_in, f32[8,32,256]{2,1,0:T(8,128)} %get-tuple-element.11.wg_in), custom_call_target="tpu_custom_call" | custom-call | tf_op jit(solution)/shard_map/pallas_call | solution.py:514
